TPU v7x, 128 devices: a whole 4x4x4 slice. The times are simulated.
128 devices in a mesh: horiz: 16 (over z, y), depth: 8 (over x, core).
Axes of the slice: x: 4, y: 4, z: 4, core: 2. Of those that a mesh axis runs over, the one named last changes fastest.
Arguments:
- source_field: float32 [64, 512, 512], P('depth', 'horiz'), may hold values from -6 to 6
- methane: float32 [64, 512, 512], P('depth', 'horiz'), may hold values from 0.2 to 1.5
- sulfate: float32 [64, 512, 512], P('depth', 'horiz'), may hold values from 0.2 to 1.5
- layer_of_cell: int32 [64], replicated, may hold values from 0 to 7
- perm_horizontal: float32 [8], replicated, may hold values from 0.3 to 3
- perm_vertical: float32 [8], replicated, may hold values from 0.3 to 3
- vent_mask: int32 [512, 512], P('horiz'), may hold values 0 or 1
Outputs:
- pressure: float32 [64, 512, 512], P('depth', 'horiz')
- methane_out: float32 [64, 512, 512], P('depth', 'horiz')
- sulfate_out: float32 [64, 512, 512], P('depth', 'horiz')
All inputs are finite; a program needn't handle non-finite values. No bound on the sum of `vent_mask` on one device may be relied on, other than what follows from the above.
Results may differ from a plain program's by a relative error of at most 0.0003.
Values sent between devices are 32-bit elements; how exact they have to be, the bound alone decides.
A program may use at most 64 MiB of HBM per device.

v0:
```python
import math

import jax
import jax.numpy as jnp
from jax import lax
from jax.sharding import PartitionSpec as P

STEPS = 4


STORAGE = 0.004
COURANT = 0.5
REACTION = 4.0
VENT_INPUT = 4.0
EXACT_PRODUCT = lax.Precision.HIGHEST


def extended(value, sides, width):
    for axis, dim in sides:
        devices, length = (lax.axis_size(axis), value.shape[dim])
        up = [(i, (i + 1) % devices) for i in range(devices)]
        down = [(j, i) for i, j in up]
        last = lax.slice_in_dim(value, length - width, length, axis=dim)
        initial = lax.slice_in_dim(value, 0, width, axis=dim)
        before = lax.ppermute(last, axis, up)
        after = lax.ppermute(initial, axis, down)
        value = jnp.concatenate([before, value, after], axis=dim)
    return value


def layer_tables(layer_of_cell, perm_horizontal, perm_vertical):
    levels = jnp.arange(perm_horizontal.shape[0], dtype=jnp.int32)
    picked = (layer_of_cell[:, None] == levels[None, :]).astype(jnp.float32)
    horizontal = jnp.sum(picked * perm_horizontal[None, :], axis=1)
    vertical = jnp.sum(picked * perm_vertical[None, :], axis=1)
    interior = 2.0 * vertical[:-1] * vertical[1:] / (vertical[:-1] + vertical[1:])
    boundary = jnp.zeros((1,), jnp.float32)
    return (horizontal, jnp.concatenate([boundary, interior, boundary]))


def eigen_values(number, offset, period):
    wave_index = (offset + jnp.arange(number, dtype=jnp.int32)) % period
    return 2.0 - 2.0 * jnp.cos(wave_index.astype(jnp.float32) * (2.0 * math.pi / period))


def dft_tables(period):
    wave_index = jnp.arange(period, dtype=jnp.int32)
    angles = (wave_index[:, None] * wave_index[None, :] % period).astype(jnp.float32) * (
        2.0 * math.pi / period
    )
    return (jnp.cos(angles), jnp.sin(angles))


def contract(form, values, table):
    return jnp.einsum(
        form, values, table, precision=EXACT_PRODUCT, preferred_element_type=jnp.float32
    )


def eliminate(upper_face, lower_face, perm_column, spectrum, f_real, f_imag, initial):

    def eliminate_advance(state_now, inputs):
        ratio_now, real_now, imag_now = state_now
        up_face, down_face, perm_value, source_real, source_imag = inputs
        pivot = up_face + down_face + perm_value * spectrum + STORAGE - up_face * ratio_now
        ratio_now = down_face / pivot
        real_now = (source_real + up_face * real_now) / pivot
        imag_now = (source_imag + up_face * imag_now) / pivot
        return ((ratio_now, real_now, imag_now), (ratio_now, real_now, imag_now))

    return lax.scan(
        eliminate_advance, initial, (upper_face, lower_face, perm_column, f_real, f_imag)
    )


def substitute(ratios, h_real, h_imag, initial):

    def substitute_advance(state_now, inputs):
        real_now, imag_now = state_now
        ratio_now, head_real, head_imag = inputs
        real_now = head_real + ratio_now * real_now
        imag_now = head_imag + ratio_now * imag_now
        return ((real_now, imag_now), (real_now, imag_now))

    _, solved = lax.scan(substitute_advance, initial, (ratios, h_real, h_imag), reverse=True)
    return solved


def upwind_divergence(rimmed_species, east_face, north_face, vertical_face):
    along_x = rimmed_species[:, 1:-1]
    flux_x = (
        jnp.maximum(east_face, 0.0) * along_x[:, :, :-1]
        + jnp.minimum(east_face, 0.0) * along_x[:, :, 1:]
    )
    centre = rimmed_species[:, 1:-1, 1:-1]
    flux_y = jnp.maximum(north_face, 0.0) * centre + jnp.minimum(north_face, 0.0) * jnp.roll(
        centre, -1, 3
    )
    along_z = rimmed_species[:, :, 1:-1]
    flux_z = (
        jnp.maximum(vertical_face, 0.0) * along_z[:, :-1]
        + jnp.minimum(vertical_face, 0.0) * along_z[:, 1:]
    )
    return (
        flux_x[:, :, 1:]
        - flux_x[:, :, :-1]
        + (flux_y - jnp.roll(flux_y, 1, 3))
        + (flux_z[:, 1:] - flux_z[:, :-1])
    )


def local(source_field, methane, sulfate, layer_of_cell, perm_horizontal, perm_vertical, vent_mask):
    depth_cells, x_local, width_y = source_field.shape
    horiz_count = lax.axis_size("horiz")
    width_x = x_local * horiz_count
    y_local = width_y // horiz_count
    horiz_index = lax.axis_index("horiz")
    depth_index = lax.axis_index("depth")
    depth_start = depth_index * depth_cells
    cos_y, sin_y = dft_tables(width_y)
    cos_x, sin_x = dft_tables(width_x)
    horizontal, face_coupling = layer_tables(layer_of_cell, perm_horizontal, perm_vertical)
    x_values = eigen_values(width_x, 0, width_x)
    y_real, y_imag = (
        contract("zxy,yk->zxk", source_field, cos_y),
        -contract("zxy,yk->zxk", source_field, sin_y),
    )
    real_part = lax.all_to_all(y_real, "horiz", split_axis=2, concat_axis=1, tiled=True)
    imag_part = lax.all_to_all(y_imag, "horiz", split_axis=2, concat_axis=1, tiled=True)
    out_real = contract("zxq,xk->zqk", real_part, cos_x) + contract("zxq,xk->zqk", imag_part, sin_x)
    out_imag = contract("zxq,xk->zqk", imag_part, cos_x) - contract("zxq,xk->zqk", real_part, sin_x)
    col_real, col_imag = (
        lax.all_to_all(out_real, "depth", split_axis=1, concat_axis=0, tiled=True),
        lax.all_to_all(out_imag, "depth", split_axis=1, concat_axis=0, tiled=True),
    )
    y_part = col_real.shape[1]
    y_values = eigen_values(y_part, horiz_index * y_local + depth_index * y_part, width_y)
    spectrum = y_values[:, None] + x_values[None, :]
    zeros_block = jnp.zeros(spectrum.shape, jnp.float32)
    _, (ratios, h_real, h_imag) = eliminate(
        face_coupling[:-1],
        face_coupling[1:],
        horizontal,
        spectrum,
        col_real,
        col_imag,
        (zeros_block, zeros_block, zeros_block),
    )
    sol_real, sol_imag = substitute(ratios, h_real, h_imag, (zeros_block, zeros_block))
    spec_real, spec_imag = (
        lax.all_to_all(sol_real, "depth", split_axis=0, concat_axis=1, tiled=True),
        lax.all_to_all(sol_imag, "depth", split_axis=0, concat_axis=1, tiled=True),
    )
    back_real = (
        contract("zqk,kx->zxq", spec_real, cos_x) - contract("zqk,kx->zxq", spec_imag, sin_x)
    ) / width_x
    back_imag = (
        contract("zqk,kx->zxq", spec_imag, cos_x) + contract("zqk,kx->zxq", spec_real, sin_x)
    ) / width_x
    back_real, back_imag = (back_real, back_imag)
    real_part = lax.all_to_all(back_real, "horiz", split_axis=1, concat_axis=2, tiled=True)
    imag_part = lax.all_to_all(back_imag, "horiz", split_axis=1, concat_axis=2, tiled=True)
    pressure = (
        contract("zxk,ky->zxy", real_part, cos_y) - contract("zxk,ky->zxy", imag_part, sin_y)
    ) / width_y
    perm_local = lax.dynamic_slice_in_dim(horizontal, depth_start, depth_cells)[:, None, None]
    face_local = lax.dynamic_slice_in_dim(face_coupling, depth_start, depth_cells + 1)[
        :, None, None
    ]
    rimmed = extended(pressure, (("horiz", 1), ("depth", 0)), 1)
    level_rows = rimmed[1:-1]
    east_face = -perm_local * (level_rows[:, 1:] - level_rows[:, :-1])
    centre = level_rows[:, 1:-1]
    north_face = -perm_local * (jnp.roll(centre, -1, 2) - centre)
    column_rows = rimmed[:, 1:-1]
    vertical_face = -face_local * (column_rows[1:] - column_rows[:-1])
    face_speed = (
        jnp.abs(east_face[:, 1:])
        + jnp.abs(east_face[:, :-1])
        + jnp.abs(north_face)
        + jnp.abs(jnp.roll(north_face, 1, 2))
        + jnp.abs(vertical_face[:-1])
        + jnp.abs(vertical_face[1:])
    )
    fastest = lax.pmax(jnp.max(face_speed), ("horiz", "depth"))
    step_size = COURANT / (fastest + 1e-06)
    vent_field = vent_mask.astype(jnp.float32)[None]
    for sweep_index in range(STEPS):
        rimmed_species = extended(jnp.stack([methane, sulfate]), (("horiz", 2), ("depth", 1)), 1)
        change = upwind_divergence(rimmed_species, east_face, north_face, vertical_face)
        reaction = REACTION * methane * sulfate
        methane_next = (
            methane - step_size * change[0] + step_size * (VENT_INPUT * vent_field - reaction)
        )
        sulfate = sulfate - step_size * change[1] - step_size * reaction
        methane = methane_next
    return (pressure, methane, sulfate)


def solution(mesh):
    in_specs = (
        P("depth", "horiz", None),
        P("depth", "horiz", None),
        P("depth", "horiz", None),
        P(),
        P(),
        P(),
        P("horiz", None),
    )
    out_specs = (P("depth", "horiz", None), P("depth", "horiz", None), P("depth", "horiz", None))
    return jax.shard_map(local, mesh=mesh, in_specs=in_specs, out_specs=out_specs, check_vma=False)
```

profile of v0, /device:TPU:7, one launch (start us, length us, event | category | flops | bytes accessed | tf_op | source)
XLA Modules:
  0.0 715.0 jit_solution(9621331607221395889)
XLA Ops:
  1.7 5.3 convolution_bitcast_fusion
  9.5 7.8 %all-to-all-start = ((f32[16,1,8192]{2,1,0:T(1,128)}), f32[16,1,8192]{2,1,0:T(1,128)S(1)}, u32[]{:S(2)}, u32[]{:S(2)}) async-start(f32[16,1,8192]{2,1,0:T(1,128)} %reshape.73), calls=%async_computation | async-start | bytes 1048576 | tf_op jit(solution)/shard_map/all_to_all | solution.py:128
  17.3 5.4 fusion.17
  27.8 4.7 all-to-all-start.1
  40.7 5.8 fusion.67
  55.0 5.5 convolution_add_fusion.1
  61.6 6.4 all-to-all-start.2
  68.0 5.3 fusion.65
  73.3 5.3 convolution_subtract_fusion.2
  79.8 4.8 all-to-all-start.3
  85.2 7.1 all-to-all-done.3
  92.9 334.5 %while.42 = (s32[]{:T(128)}, f32[4,512]{1,0:T(4,128)S(1)}, f32[4,512]{1,0:T(4,128)S(1)}, f32[4,512]{1,0:T(4,128)S(1)}, f32[64,4,512]{2,1,0:T(4,128)S(1)}, /*inde...) while((s32[]{:T(128)}, f32[4,512]{1,0:T(4,128)S(1)}, ...), condition=%wide.region_3.4_spmd.clone, body=%wide.region_2.3_spmd.clone.sunk | while | flops 32772 | bytes 92907 | solution.py:71
  428.4 39.0 %while.43 = (s32[]{:T(128)}, f32[4,512]{1,0:T(4,128)S(1)}, f32[4,512]{1,0:T(4,128)S(1)}, f32[64,4,512]{2,1,0:T(4,128)}, f32[64,4,512]{2,1,0:T(4,128)S(1)}, /*ind...) while((s32[]{:T(128)}, f32[4,512]{1,0:T(4,128)S(1)}, ...), condition=%wide.region_5.6_spmd.clone, body=%wide.region_4.5_spmd.clone.sunk | while | flops 12292 | bytes 73871 | solution.py:85
  467.4 12.7 %all_to_all.144 = f32[64,4,512]{2,1,0:T(4,128)S(1)} all-to-all(f32[64,4,512]{2,1,0:T(4,128)S(1)} %get-tuple-element.237), channel_id=1, replica_groups=mesh['horiz'=16,'depth'=8] {'depth'}, dimensions={0} | all-to-all | bytes 1048576 | tf_op jit(solution)/shard_map/all_to_all | solution.py:152
  480.2 6.2 all-to-all-start.4
  488.1 3.9 collective-permute-start.5
  494.7 5.4 fusion.59
  500.1 5.9 fusion.15
  509.5 6.7 all-to-all-start.7
  516.2 6.4 fusion.63
  522.7 5.9 fusion.13
  532.1 6.8 all-to-all-start.6
  543.3 3.7 reduce.3
  554.3 3.7 reduce.2
  564.7 5.3 fusion.61
  570.0 5.5 fusion.16
  590.0 65.2 %pmax.7 = f32[]{:T(128)} all-reduce(f32[]{:T(128)} %get-tuple-element.409), channel_id=1, replica_groups=mesh['horiz'=16,'depth'=8] {'horiz','depth'}, use_global_device_ids=true, to_apply=%region_7.8 | all-reduce | flops 1 | bytes 8 | tf_op jit(solution)/shard_map/pmax | solution.py:185
  665.6 4.0 collective-permute-start.9
  670.7 4.3 collective-permute-start.10
  683.1 5.4 collective-permute-start.13
  692.9 3.7 collective-permute-done.15
  698.7 5.2 collective-permute-start.17
  (504 shorter events, 398.5 us)
Async XLA Ops:
  9.5 18.3 %all-to-all-start = ((f32[16,1,8192]{2,1,0:T(1,128)}), f32[16,1,8192]{2,1,0:T(1,128)S(1)}, u32[]{:S(2)}, u32[]{:S(2)}) async-start(f32[16,1,8192]{2,1,0:T(1,128)} %reshape.73), calls=%async_computation | async-start | bytes 1048576 | tf_op jit(solution)/shard_map/all_to_all | solution.py:128
  23.4 9.1 %copy-start.18 = (f32[8]{0:T(128)S(1)}, f32[8]{0:T(128)}, u32[]{:S(2)}) copy-start(f32[8]{0:T(128)} %param.15) | copy-start | bytes 100
  23.5 9.1 %copy-start.19 = (s32[64]{0:T(128)S(1)}, s32[64]{0:T(128)}, u32[]{:S(2)}) copy-start(s32[64]{0:T(128)} %param.14) | copy-start | bytes 772
  27.8 18.6 %all-to-all-start.1 = ((f32[16,1,8192]{2,1,0:T(1,128)}), f32[16,1,8192]{2,1,0:T(1,128)}, u32[]{:S(2)}, u32[]{:S(2)}) async-start(f32[16,1,8192]{2,1,0:T(1,128)} %reshape.75), calls=%async_computation.1 | async-start | bytes 1048576 | tf_op jit(solution)/shard_map/all_to_all | solution.py:129
  61.6 18.2 %all-to-all-start.2 = ((f32[8,32,512]{2,0,1:T(8,128)}), f32[8,32,512]{2,0,1:T(8,128)S(1)}, u32[]{:S(2)}, u32[]{:S(2)}) async-start(f32[8,32,512]{2,0,1:T(8,128)} %copy.36), calls=%async_computation.2 | async-start | bytes 1048576 | tf_op jit(solution)/shard_map/all_to_all | solution.py:133
  79.8 12.6 %all-to-all-start.3 = ((f32[8,32,512]{2,0,1:T(8,128)}), f32[8,32,512]{2,0,1:T(8,128)S(1)}, u32[]{:S(2)}, u32[]{:S(2)}) async-start(f32[8,32,512]{2,0,1:T(8,128)} %copy.38), calls=%async_computation.3 | async-start | bytes 1048576 | tf_op jit(solution)/shard_map/all_to_all | solution.py:134
  467.4 18.9 %copy-start.2 = (f32[8,32,512]{2,1,0:T(8,128)S(1)}, f32[8,32,512]{2,1,0:T(8,128)}, u32[]{:S(2)}) copy-start(f32[8,32,512]{2,1,0:T(8,128)} %param.13) | copy-start | bytes 1572868
  467.4 18.9 %copy-start.3 = (f32[8,32,512]{2,1,0:T(8,128)S(1)}, f32[8,32,512]{2,1,0:T(8,128)}, u32[]{:S(2)}) copy-start(f32[8,32,512]{2,1,0:T(8,128)} %param.12) | copy-start | bytes 1572868
  480.2 14.3 %all-to-all-start.4 = ((f32[64,4,512]{2,1,0:T(4,128)}), f32[64,4,512]{2,1,0:T(4,128)S(1)}, u32[]{:S(2)}, u32[]{:S(2)}) async-start(f32[64,4,512]{2,1,0:T(4,128)} %get-tuple-element.236), calls=%async_computation.4 | async-start | bytes 1048576 | tf_op jit(solution)/shard_map/all_to_all | solution.py:151
  486.4 52.7 %collective-permute-start.4 = (f32[2,8,1,512]{3,2,1,0:T(1,128)S(1)}, f32[2,8,1,512]{3,2,1,0:T(1,128)S(1)}, u32[]{:S(2)}, u32[]{:S(2)}) collective-permute-start(f32[2,8,1,512]{3,2,1,0:T(1,128)S(1)} %get-tuple-element.402), channel_id=1, source_target_pairs={{0,8},{8,16},{16,24},{24,32},{32,40},{40,48},{48,56},{56,64},{64,7... | collective-permute-start | bytes 98312 | tf_op jit(solution)/shard_map/ppermute | solution.py:25
  488.1 51.0 %collective-permute-start.5 = (f32[2,8,1,512]{3,2,1,0:T(1,128)S(1)}, f32[2,8,1,512]{3,2,1,0:T(1,128)S(1)}, u32[]{:S(2)}, u32[]{:S(2)}) collective-permute-start(f32[2,8,1,512]{3,2,1,0:T(1,128)S(1)} %get-tuple-element.403), channel_id=1, source_target_pairs={{8,0},{16,8},{24,16},{32,24},{40,32},{48,40},{56,48},{64,56},{72,6... | collective-permute-start | bytes 98312 | tf_op jit(solution)/shard_map/ppermute | solution.py:26
  509.5 22.6 %all-to-all-start.7 = ((f32[16,1,8192]{2,1,0:T(1,128)}), f32[16,1,8192]{2,1,0:T(1,128)}, u32[]{:S(2)}, u32[]{:S(2)}) async-start(f32[16,1,8192]{2,1,0:T(1,128)} %reshape.79), calls=%async_computation.7 | async-start | bytes 1048576 | tf_op jit(solution)/shard_map/all_to_all | solution.py:162
  532.1 22.2 %all-to-all-start.6 = ((f32[16,1,8192]{2,1,0:T(1,128)}), f32[16,1,8192]{2,1,0:T(1,128)}, u32[]{:S(2)}, u32[]{:S(2)}) async-start(f32[16,1,8192]{2,1,0:T(1,128)} %reshape.77), calls=%async_computation.6 | async-start | bytes 1048576 | tf_op jit(solution)/shard_map/all_to_all | solution.py:161
  539.9 120.7 %collective-permute-start.6 = (f32[2,1,34,512]{3,2,1,0:T(8,128)}, f32[2,1,34,512]{3,2,1,0:T(8,128)}, u32[]{:S(2)}, u32[]{:S(2)}) collective-permute-start(f32[2,1,34,512]{3,2,1,0:T(8,128)} %get-tuple-element.394), channel_id=1, source_target_pairs={{0,1},{1,2},{2,3},{3,4},{4,5},{5,6},{6,7},{7,0},{8,9},{9,10},{10,1... | collective-permute-start | bytes 417800 | tf_op jit(solution)/shard_map/ppermute | solution.py:25
  543.3 117.3 %collective-permute-start.7 = (f32[2,1,34,512]{3,2,1,0:T(8,128)}, f32[2,1,34,512]{3,2,1,0:T(8,128)}, u32[]{:S(2)}, u32[]{:S(2)}) collective-permute-start(f32[2,1,34,512]{3,2,1,0:T(8,128)} %get-tuple-element.395), channel_id=1, source_target_pairs={{1,0},{2,1},{3,2},{4,3},{5,4},{6,5},{7,6},{0,7},{9,8},{10,9},{11,1... | collective-permute-start | bytes 417800 | tf_op jit(solution)/shard_map/ppermute | solution.py:26
  575.5 12.5 %copy-start.4 = (f32[8,32,512]{2,1,0:T(8,128)}, f32[8,32,512]{2,1,0:T(8,128)S(1)}, u32[]{:S(2)}) copy-start(f32[8,32,512]{2,1,0:T(8,128)S(1)} %fusion.16) | copy-start | bytes 1572868
  575.8 6.3 collective-permute-start.1
  577.6 4.5 collective-permute-start
  582.1 6.0 collective-permute-start.2
  583.0 5.0 collective-permute-start.3
  664.5 6.2 collective-permute-start.8
  665.6 5.1 collective-permute-start.9
  670.7 6.6 collective-permute-start.10
  675.0 6.0 collective-permute-start.11
  683.0 6.7 collective-permute-start.12
  683.1 6.6 collective-permute-start.13
  689.7 3.1 collective-permute-start.14
  690.6 6.0 collective-permute-start.15
  698.6 6.5 collective-permute-start.16
  698.7 6.4 collective-permute-start.17
  705.2 3.1 collective-permute-start.18
  706.0 6.0 collective-permute-start.19
  (17 other events, 59.7 us)
where the time goes:
time: 726 us; the launch traced here: 715 us
  other arithmetic  203 us (28%)
  local copies, waits for them, and re-layouts  167 us (23%)
  loops' own time  84.4 us (12%)
  starting transfers between devices  83.4 us (11%)
  blocking collectives  77.9 us (11%)
  matrix products  67.1 us (9%)
  waiting for transfers between devices  29.7 us (4%)
    dynamic_update_slice x128, other arithmetic, eliminate(): lax.scan(eliminate_advance, initial, (upper_face, lower_face, perm_column...  169 us
    dynamic_slice x192, local copies, waits for them, and re-layouts, eliminate(): lax.scan(eliminate_advance, initial, (upper_face, lower_face, perm_column...  120 us
    another operation x1, loops' own time, eliminate(): lax.scan(eliminate_advance, initial, (upper_face, lower_face, perm_column...  84.4 us
    dot_general x12, matrix products, contract(): jnp.einsum(form, values, table, precision=EXACT_PRODUCT, preferred_elemen...  67.1 us
    pmax x1, blocking collectives, local(): fastest = lax.pmax(jnp.max(face_speed), ('horiz', 'depth'))  65.2 us
    ppermute x10, starting transfers between devices, extended(): after = lax.ppermute(initial, axis, down)  22.8 us
    ppermute x10, starting transfers between devices, extended(): before = lax.ppermute(last, axis, up)  17.2 us
  transfers between devices with their start and end apart: 27, of which 13 were waited for; matrix products, arithmetic and copies ran while one was open for 14% of the time, Pallas kernels for 0%

commit v1 on v0

v1 whole, which is shorter than its diff:
```python
import functools

import jax
import jax.numpy as jnp
import ml_dtypes
import numpy as np
from jax import lax
from jax.experimental import pallas as pl
from jax.experimental.pallas import tpu as pltpu
from jax.sharding import PartitionSpec as P

STEPS = 4
STORAGE = 0.004
COURANT = 0.5
REACTION = 4.0
VENT_INPUT = 4.0

NZ = 64
N = 512
NH = 16
ND = 8
ZL = 8
XL = 32
HALO = 4
ZE = ZL + 2 * HALO
XE = XL + 16
NB = NZ // 2

F32 = jnp.float32
BF16 = jnp.bfloat16


def tables():
    k = np.arange(N)
    angle = (k[:, None] * k[None, :] % N) * (2.0 * np.pi / N)
    cas = np.cos(angle) + np.sin(angle)
    hi = cas.astype(np.float32).astype(ml_dtypes.bfloat16)
    lo = (cas - hi.astype(np.float64)).astype(np.float32).astype(ml_dtypes.bfloat16)
    eig = (4.0 * np.sin(np.pi * k / N) ** 2).astype(np.float32)
    eig_x = np.broadcast_to(eig.reshape(NB, 16, 1), (NB, 16, 128)).copy()
    eig_y = np.broadcast_to(eig.reshape(4, 1, 128), (4, 16, 128)).copy()
    return hi, lo, eig_x, eig_y


def split(v):
    hi = v.astype(BF16)
    return hi, (v - hi.astype(F32)).astype(BF16)


def dot3(a, b):
    (ah, al), (bh, bl) = a, b
    d = functools.partial(jnp.dot, preferred_element_type=F32)
    return d(ah, bh) + (d(al, bh) + d(ah, bl))


def kernel(
    src, met, sul, layer, ph, pv, vent, hhi, hlo, eig_x, eig_y,
    out_p, out_m, out_s,
    y1, r1, zb, cb, r3, xb, y4,
    inv, ci, rat,
    ep, em, es, em2, es2, ev, pack, xin, coef, tend,
    mx, mxh, mxd, cpl, khs,
    s1, q1, s2, q2, s3, q3, s4, q4, hs, hq, vs, vq, ms, mq, ns, nq, lsem,
):
    h = lax.axis_index("horiz")
    d = lax.axis_index("depth")
    qb = lax.div(h, 4)
    qa = lax.rem(h, 4)
    b = d * 4 + qb

    def dev(hh, dd):
        return {"horiz": hh, "depth": dd}

    def mate(j):
        return lax.rem(h + j, NH)

    def fellow(j):
        pb = lax.rem(b + j, NB)
        return pb, lax.rem(pb, 4) * 4 + qa, lax.div(pb, 4)

    h_up, h_dn = lax.rem(h + 1, NH), lax.rem(h + NH - 1, NH)
    d_up, d_dn = lax.rem(d + 1, ND), lax.rem(d + ND - 1, ND)

    own_copies = [
        pltpu.make_async_copy(met, em.at[pl.ds(HALO, ZL), pl.ds(8, XL)], lsem.at[0]),
        pltpu.make_async_copy(sul, es.at[pl.ds(HALO, ZL), pl.ds(8, XL)], lsem.at[1]),
    ]
    for c in own_copies:
        c.start()

    barrier = pltpu.get_barrier_semaphore()

    def greet_h(j, _):
        pl.semaphore_signal(barrier, inc=1, device_id=dev(mate(j), d))
        return 0

    def greet_b(j, _):
        _, fh, fd = fellow(j)
        pl.semaphore_signal(barrier, inc=1, device_id=dev(fh, fd))
        return 0

    lax.fori_loop(1, NH, greet_h, 0)
    lax.fori_loop(1, NB, greet_b, 0)
    for hh in (h_up, h_dn):
        for dd in (d_up, d_dn):
            pl.semaphore_signal(barrier, inc=1, device_id=dev(hh, dd))

    def table(z, _):
        khs[z] = ph[layer[z]]
        return 0

    lax.fori_loop(0, NZ, table, 0)
    cpl[0] = 0.0
    cpl[NZ] = 0.0

    def face(i, _):
        a, c = pv[layer[i - 1]], pv[layer[i]]
        cpl[i] = 2.0 * a * c / (a + c)
        return 0

    lax.fori_loop(1, NZ, face, 0)

    hh_, hl_ = hhi[...], hlo[...]
    table_h = (hh_, hl_)
    s = split(src[...].reshape(ZL * XL, N))
    for n in range(2):
        cols = (hhi[:, 256 * n:256 * n + 256], hlo[:, 256 * n:256 * n + 256])
        o = dot3(s, cols)
        y1[2 * n] = o[:, :128].reshape(ZL, XL, 128)
        y1[2 * n + 1] = o[:, 128:].reshape(ZL, XL, 128)

    pl.semaphore_wait(barrier, (NH - 1) + (NB - 1) + 4)

    def copy1(j, origin):
        peer = mate(j)
        return pltpu.make_async_remote_copy(
            src_ref=y1.at[lax.rem(peer, 4), pl.ds(2 * lax.div(peer, 4), 2)],
            dst_ref=r1.at[:, pl.ds(pl.multiple_of(XL * origin, XL), XL), :],
            send_sem=s1.at[j], recv_sem=q1.at[j], device_id=dev(peer, d))

    def go1(j, _):
        copy1(j, h).start()
        return 0

    lax.fori_loop(1, NH, go1, 0)

    def halo_copies(f, ref, dirs):
        own = pl.ds(8, XL)
        lo_p, hi_p = pack.at[f, 0], pack.at[f, 1]
        plan = (
            (ref.at[pl.ds(8, 4), own], ref.at[pl.ds(0, 4), own], h, d_up),
            (ref.at[pl.ds(4, 4), own], ref.at[pl.ds(12, 4), own], h, d_dn),
            (hi_p, xin.at[f, 0, pl.ds(2, 4)], h_up, d),
            (lo_p, xin.at[f, 1, pl.ds(2, 4)], h_dn, d),
            (hi_p.at[pl.ds(2, 2)], xin.at[f, 0, pl.ds(0, 2)], h_up, d_up),
            (hi_p.at[pl.ds(0, 2)], xin.at[f, 0, pl.ds(6, 2)], h_up, d_dn),
            (lo_p.at[pl.ds(2, 2)], xin.at[f, 1, pl.ds(0, 2)], h_dn, d_up),
            (lo_p.at[pl.ds(0, 2)], xin.at[f, 1, pl.ds(6, 2)], h_dn, d_dn),
        )
        return [
            pltpu.make_async_remote_copy(
                src_ref=plan[i][0], dst_ref=plan[i][1], send_sem=hs.at[f, i], recv_sem=hq.at[f, i],
                device_id=dev(plan[i][2], plan[i][3]))
            for i in dirs
        ]

    sub8 = lax.broadcasted_iota(jnp.int32, (8, N), 0)

    def pack_rows(f, ref):
        for zz in range(ZL // 2):
            even, odd = ref[HALO + 2 * zz], ref[HALO + 2 * zz + 1]
            pack[f, 0, zz] = jnp.where(sub8 < 4, even[8:16], pltpu.roll(odd[8:16], 4, 0))
            pack[f, 1, zz] = jnp.where(sub8 >= 4, even[32:40], pltpu.roll(odd[32:40], 4, 0))

    def unpack_rows(f, ref):
        for zz in range(ZE // 2):
            for side, row in ((0, 0), (1, 40)):
                tile = xin[f, side, zz]
                ref[2 * zz, row:row + 8] = tile
                ref[2 * zz + 1, row:row + 8] = pltpu.roll(tile, 4, 0)

    for c in own_copies:
        c.wait()
    conc = ((1, em), (2, es))
    for f, ref in conc:
        for c in halo_copies(f, ref, (0, 1)):
            c.start()
    for f, ref in conc:
        pack_rows(f, ref)
    ev[8:40] = vent[...].astype(F32)
    vent_copies = [
        pltpu.make_async_remote_copy(
            src_ref=ev.at[pl.ds(32, 8)], dst_ref=ev.at[pl.ds(0, 8)],
            send_sem=vs.at[0], recv_sem=vq.at[0], device_id=dev(h_up, d)),
        pltpu.make_async_remote_copy(
            src_ref=ev.at[pl.ds(8, 8)], dst_ref=ev.at[pl.ds(40, 8)],
            send_sem=vs.at[1], recv_sem=vq.at[1], device_id=dev(h_dn, d)),
    ]

    lam = eig_x[b] + eig_y[qa]

    def factor(z, r):
        cu, cd = cpl[z], cpl[z + 1]
        den = (cu + cd + khs[z] * lam + STORAGE) - cu * r
        i = 1.0 / den
        r = cd * i
        inv[z] = i
        ci[z] = cu * i
        rat[z] = r
        return r

    lax.fori_loop(0, NZ, factor, jnp.zeros((16, 128), F32))

    own_x = pl.ds(pl.multiple_of(XL * h, XL), XL)
    r1[:, own_x, :] = y1[qa, pl.ds(2 * qb, 2)]

    def done1(j, _):
        copy1(j, lax.rem(h + NH - j, NH)).wait_recv()
        return 0

    lax.fori_loop(1, NH, done1, 0)

    o = dot3(table_h, split(jnp.concatenate([r1[0], r1[1]], axis=1)))
    zb[0] = o[:, :128]
    zb[1] = o[:, 128:]

    def copy2(j, origin):
        pb, fh, fd = fellow(j)
        return pltpu.make_async_remote_copy(
            src_ref=zb.at[:, pl.ds(pl.multiple_of(16 * pb, 16), 16), :],
            dst_ref=cb.at[pl.ds(2 * origin, 2)],
            send_sem=s2.at[j], recv_sem=q2.at[j], device_id=dev(fh, fd))

    def go2(j, _):
        copy2(j, b).start()
        return 0

    lax.fori_loop(1, NB, go2, 0)
    for f, ref in conc:
        for c in halo_copies(f, ref, range(2, 8)):
            c.start()
    for c in vent_copies:
        c.start()
    own_k = pl.ds(pl.multiple_of(16 * b, 16), 16)
    cb[pl.ds(2 * b, 2)] = zb[:, own_k, :]

    def done2(j, _):
        copy2(j, lax.rem(b + NB - j, NB)).wait_recv()
        return 0

    lax.fori_loop(1, NB, done2, 0)

    def down(z, hz):
        hz = cb[z] * (inv[z] * (1.0 / (N * N))) + ci[z] * hz
        cb[z] = hz
        return hz

    lax.fori_loop(0, NZ, down, jnp.zeros((16, 128), F32), unroll=8)

    def up(i, p):
        z = NZ - 1 - i
        p = cb[z] + rat[z] * p
        cb[z] = p
        return p

    lax.fori_loop(0, NZ, up, jnp.zeros((16, 128), F32), unroll=8)

    def copy3(j, origin):
        pb, fh, fd = fellow(j)
        return pltpu.make_async_remote_copy(
            src_ref=cb.at[pl.ds(2 * pb, 2)],
            dst_ref=r3.at[:, pl.ds(pl.multiple_of(16 * origin, 16), 16), :],
            send_sem=s3.at[j], recv_sem=q3.at[j], device_id=dev(fh, fd))

    def go3(j, _):
        copy3(j, b).start()
        return 0

    lax.fori_loop(1, NB, go3, 0)
    r3[:, own_k, :] = cb[pl.ds(2 * b, 2)]

    def done3(j, _):
        copy3(j, lax.rem(b + NB - j, NB)).wait_recv()
        return 0

    lax.fori_loop(1, NB, done3, 0)

    o = dot3(table_h, split(jnp.concatenate([r3[0], r3[1]], axis=1)))
    xb[0] = o[:, :128]
    xb[1] = o[:, 128:]

    def copy4(j, oa, ob):
        peer = mate(j)
        return pltpu.make_async_remote_copy(
            src_ref=xb.at[:, pl.ds(pl.multiple_of(XL * peer, XL), XL), :],
            dst_ref=y4.at[oa, pl.ds(2 * ob, 2)],
            send_sem=s4.at[j], recv_sem=q4.at[j], device_id=dev(peer, d))

    def go4(j, _):
        copy4(j, qa, qb).start()
        return 0

    lax.fori_loop(1, NH, go4, 0)
    y4[qa, pl.ds(2 * qb, 2)] = xb[:, own_x, :]

    for f, ref in conc:
        for c in halo_copies(f, ref, range(8)):
            c.wait()
        unpack_rows(f, ref)
    for c in vent_copies:
        c.wait()

    def done4(j, _):
        origin = lax.rem(h + NH - j, NH)
        copy4(j, lax.rem(origin, 4), lax.div(origin, 4)).wait_recv()
        return 0

    lax.fori_loop(1, NH, done4, 0)

    s = split(jnp.concatenate([y4[k].reshape(ZL * XL, 128) for k in range(4)], axis=1))
    for n in range(2):
        o = dot3(s, (hhi[:, 256 * n:256 * n + 256], hlo[:, 256 * n:256 * n + 256]))
        ep[HALO:HALO + ZL, 8:40, 256 * n:256 * n + 256] = o.reshape(ZL, XL, 256)
    out_p[...] = ep[HALO:HALO + ZL, 8:40, :]

    pack_rows(0, ep)
    p_halo = halo_copies(0, ep, range(8))
    for c in p_halo:
        c.start()
    for c in p_halo:
        c.wait_recv()
    unpack_rows(0, ep)

    def cell(i):
        gz = lax.rem(d * ZL + i + (NZ - HALO), NZ)
        kh, cu, cd = khs[gz], cpl[gz], cpl[gz + 1]
        p = ep[i]
        east = -kh * (pltpu.roll(p, XE - 1, 0) - p)
        north = -kh * (pltpu.roll(p, N - 1, 1) - p)
        above = -cu * (p - ep[i - 1])
        below = -cd * (ep[i + 1] - p)
        return east, pltpu.roll(east, 1, 0), north, pltpu.roll(north, 1, 1), above, below

    def speed(i, m):
        e, w, n, s_, a, c = [jnp.abs(v[8:40]) for v in cell(i)]
        v = e + w + n + s_ + a + c
        v = jnp.max(v.reshape(4, 8, N), axis=0)
        return jnp.maximum(m, jnp.maximum(jnp.maximum(v[:, :128], v[:, 128:256]),
                                          jnp.maximum(v[:, 256:384], v[:, 384:])))

    mx[0] = lax.fori_loop(HALO, HALO + ZL, speed, jnp.zeros((8, 128), F32))

    def copy_m(j, origin):
        return pltpu.make_async_remote_copy(
            src_ref=mx.at[0], dst_ref=mxh.at[origin], send_sem=ms.at[j], recv_sem=mq.at[j],
            device_id=dev(mate(j), d))

    def copy_n(j, origin):
        return pltpu.make_async_remote_copy(
            src_ref=mx.at[1], dst_ref=mxd.at[origin], send_sem=ns.at[j], recv_sem=nq.at[j],
            device_id=dev(h, lax.rem(d + j, ND)))

    def go_m(j, _):
        copy_m(j, h).start()
        return 0

    lax.fori_loop(1, NH, go_m, 0)
    mxh[h] = mx[0]

    def stencil(get, c_ref, i):
        c = c_ref[i]
        return (get(0) * c
                + get(1) * pltpu.roll(c, XE - 1, 0) + get(2) * pltpu.roll(c, 1, 0)
                + get(3) * pltpu.roll(c, N - 1, 1) + get(4) * pltpu.roll(c, 1, 1)
                + get(5) * c_ref[i + 1] + get(6) * c_ref[i - 1])

    def tendencies(m_ref, s_ref, i):
        get = lambda k: coef[k, i - 1]
        react = REACTION * m_ref[i] * s_ref[i]
        return (stencil(get, m_ref, i) + (react - VENT_INPUT * ev[...]),
                stencil(get, s_ref, i) + react)

    def prepare(i, _):
        e, w, n, s_, a, c = cell(i)
        pos, neg = (lambda v: jnp.maximum(v, 0.0)), (lambda v: jnp.minimum(v, 0.0))
        coef[0, i - 1] = (pos(e) - neg(w)) + (pos(n) - neg(s_)) + (pos(c) - neg(a))
        coef[1, i - 1] = neg(e)
        coef[2, i - 1] = -pos(w)
        coef[3, i - 1] = neg(n)
        coef[4, i - 1] = -pos(s_)
        coef[5, i - 1] = neg(c)
        coef[6, i - 1] = -pos(a)
        t_m, t_s = tendencies(em, es, i)
        tend[0, i - 1] = t_m
        tend[1, i - 1] = t_s
        return 0

    lax.fori_loop(1, 8, prepare, 0)

    def done_m(j, _):
        copy_m(j, lax.rem(h + NH - j, NH)).wait_recv()
        return 0

    lax.fori_loop(1, NH, done_m, 0)
    mx[1] = jnp.max(mxh[...], axis=0)

    def go_n(j, _):
        copy_n(j, d).start()
        return 0

    lax.fori_loop(1, ND, go_n, 0)
    mxd[d] = mx[1]

    lax.fori_loop(8, ZE - 1, prepare, 0)

    def done_n(j, _):
        copy_n(j, lax.rem(d + ND - j, ND)).wait_recv()
        return 0

    lax.fori_loop(1, ND, done_n, 0)
    fastest = jnp.max(jnp.max(mxd[...], axis=0), axis=(0, 1), keepdims=True)
    dt = COURANT / (fastest + 1e-6)

    def first(i, _):
        em2[i] = em[i] - dt * tend[0, i - 1]
        es2[i] = es[i] - dt * tend[1, i - 1]
        return 0

    lax.fori_loop(1, ZE - 1, first, 0)

    def step(a, c, lo):
        def body(i, _):
            t_m, t_s = tendencies(a[0], a[1], i)
            c[0][i] = a[0][i] - dt * t_m
            c[1][i] = a[1][i] - dt * t_s
            return 0

        lax.fori_loop(lo, ZE - lo, body, 0)

    step((em2, es2), (em, es), 2)
    step((em, es), (em2, es2), 3)

    def last(i, _):
        t_m, t_s = tendencies(em2, es2, i)
        out_m[i - HALO] = (em2[i] - dt * t_m)[8:40]
        out_s[i - HALO] = (es2[i] - dt * t_s)[8:40]
        return 0

    lax.fori_loop(HALO, HALO + ZL, last, 0)

    def left_h(j, _):
        copy1(j, h).wait_send()
        copy4(j, qa, qb).wait_send()
        copy_m(j, h).wait_send()
        return 0

    def left_b(j, _):
        copy2(j, b).wait_send()
        copy3(j, b).wait_send()
        return 0

    def left_d(j, _):
        copy_n(j, d).wait_send()
        return 0

    lax.fori_loop(1, NH, left_h, 0)
    lax.fori_loop(1, NB, left_b, 0)
    lax.fori_loop(1, ND, left_d, 0)
    for c in p_halo:
        c.wait_send()


def local(source_field, methane, sulfate, layer_of_cell, perm_horizontal, perm_vertical, vent_mask):
    hi, lo, eig_x, eig_y = tables()
    vmem = pl.BlockSpec(memory_space=pltpu.VMEM)
    smem = pl.BlockSpec(memory_space=pltpu.SMEM)
    hbm = pl.BlockSpec(memory_space=pl.ANY)
    field = jax.ShapeDtypeStruct((ZL, XL, N), F32)
    dma = pltpu.SemaphoreType.DMA
    ext = pltpu.VMEM((ZE, XE, N), F32)
    scratch = [
        pltpu.VMEM((4, ZL, XL, 128), F32),
        pltpu.VMEM((2, N, 128), F32),
        pltpu.VMEM((2, N, 128), F32),
        pltpu.VMEM((NZ, 16, 128), F32),
        pltpu.VMEM((2, N, 128), F32),
        pltpu.VMEM((2, N, 128), F32),
        pltpu.VMEM((4, ZL, XL, 128), F32),
        pltpu.VMEM((NZ, 16, 128), F32),
        pltpu.VMEM((NZ, 16, 128), F32),
        pltpu.VMEM((NZ, 16, 128), F32),
        ext, ext, ext, ext, ext,
        pltpu.VMEM((XE, N), F32),
        pltpu.VMEM((3, 2, ZL // 2, 8, N), F32),
        pltpu.VMEM((3, 2, ZE // 2, 8, N), F32),
        pltpu.VMEM((7, ZE - 2, XE, N), F32),
        pltpu.VMEM((2, ZE - 2, XE, N), F32),
        pltpu.VMEM((2, 8, 128), F32),
        pltpu.VMEM((NH, 8, 128), F32),
        pltpu.VMEM((ND, 8, 128), F32),
        pltpu.SMEM((NZ + 1,), F32),
        pltpu.SMEM((NZ,), F32),
        dma((NH,)), dma((NH,)), dma((NB,)), dma((NB,)), dma((NB,)), dma((NB,)), dma((NH,)), dma((NH,)),
        dma((3, 8)), dma((3, 8)), dma((2,)), dma((2,)),
        dma((NH,)), dma((NH,)), dma((ND,)), dma((ND,)), dma((2,)),
    ]
    return pl.pallas_call(
        kernel,
        out_shape=(field, field, field),
        in_specs=[vmem, hbm, hbm, smem, smem, smem, vmem, vmem, vmem, vmem, vmem],
        out_specs=(vmem, vmem, vmem),
        scratch_shapes=scratch,
        compiler_params=pltpu.CompilerParams(
            collective_id=0, has_side_effects=True, vmem_limit_bytes=60 * 1024 * 1024),
    )(source_field, methane, sulfate, layer_of_cell, perm_horizontal, perm_vertical, vent_mask,
      jnp.asarray(hi), jnp.asarray(lo), jnp.asarray(eig_x), jnp.asarray(eig_y))


def solution(mesh):
    field = P("depth", "horiz", None)
    return jax.shard_map(
        local,
        mesh=mesh,
        in_specs=(field, field, field, P(), P(), P(), P("horiz", None)),
        out_specs=(field, field, field),
        check_vma=False,
    )
```

time: 726 us -> 85 us (0.12)
  the two profiles are of different devices: /device:TPU:7 before, /device:TPU:1 now
where the time goes in v1:
time: 85 us; the launch traced here: 84.8 us
  Pallas kernels  80.2 us (94%)
  local copies, waits for them, and re-layouts  3.95 us (5%)
    pallas_call x1, Pallas kernels, local(): pl.pallas_call(kernel, out_shape=(field, field, field), in_specs=[vmem, h...  80.2 us
    unnamed x7, local copies, waits for them, and re-layouts  3.95 us

profile of v1, /device:TPU:1, one launch (start us, length us, event | category | flops | bytes accessed | tf_op | source)
XLA Modules:
  0.0 84.8 jit_solution(9067330408637765494)
XLA Ops:
  0.6 80.2 %shard_map.130 = (f32[8,32,512]{2,1,0:T(8,128)}, f32[8,32,512]{2,1,0:T(8,128)}, f32[8,32,512]{2,1,0:T(8,128)}) custom-call(f32[8,32,512]{2,1,0:T(8,128)} %src.1, f32[8,32,512]{2,1,0:T(8,128)} %met.1, f32[8,32,512]{2,1,0:T(8,128)} %sul.1, s32[64]{0:T(128)} %layer.1, f32[8]{0:T(128)} %ph.1, f32[8]{0:T(128)} %pv.1, s32[32,512]{1,0:T(8,128)} %vent.1, ...), custom_call_target="tpu_custom_call" | custom-call | tf_op jit(solution)/shard_map/pallas_call | solution.py:507
  80.8 0.0 copy-start.1
  80.8 1.9 %copy.17 = f32[8,32,512]{2,1,0:T(8,128)} copy(f32[8,32,512]{2,1,0:T(8,128)} %get-tuple-element.6) | data formatting | bytes 1048576
  82.7 0.0 copy-done.1
  82.7 0.0 copy-start
  82.7 0.8 copy.18
  83.5 0.4 copy-done
  84.0 0.8 copy.19
Async XLA Ops:
  80.8 1.9 %copy-start.1 = (f32[8,32,512]{2,1,0:T(8,128)S(1)}, f32[8,32,512]{2,1,0:T(8,128)}, u32[]{:S(2)}) copy-start(f32[8,32,512]{2,1,0:T(8,128)} %get-tuple-element.7) | copy-start | bytes 1572868
  82.7 1.2 %copy-start = (f32[8,32,512]{2,1,0:T(8,128)S(1)}, f32[8,32,512]{2,1,0:T(8,128)}, u32[]{:S(2)}) copy-start(f32[8,32,512]{2,1,0:T(8,128)} %get-tuple-element.8) | copy-start | bytes 1572868
